TPU v7x, 512 devices: a whole 4x8x8 slice. The times are simulated.
512 devices in a mesh: tm: 4 (over x), rows: 128 (over z, y, core).
Axes of the slice: x: 4, y: 8, z: 8, core: 2. Of those that a mesh axis runs over, the one named last changes fastest.
Arguments:
- frames: bfloat16 [16, 1024, 64, 128], P('tm', 'rows'), may hold values from -50 to 50
- video_pos: int32 [16], P('tm'), may hold values from 0 to 3, as said below
- norm1_gain: float32 [128], replicated, may hold values from 0.25 to 1.75
- norm1_shift: float32 [128], replicated, may hold values from -3 to 3
- conv1_weight: bfloat16 [3, 3, 3, 128, 128], replicated, may hold values from -0.109375 to 0.109375
- norm2_gain: float32 [128], replicated, may hold values from 0.25 to 1.75
- norm2_shift: float32 [128], replicated, may hold values from -3 to 3
- conv2_weight: bfloat16 [3, 3, 3, 128, 128], replicated, may hold values from -0.109375 to 0.109375
Outputs:
- encoded: bfloat16 [16, 1024, 64, 128], P('tm', 'rows')
Inputs may be any that keep to these rules, and one draw needn't show every extreme that they name: video_pos[0] = 0, and each later frame's value is 0 (a new video begins) or one more than the previous frame's; a video begins only at frame 0 and at frames whose index modulo 4 is 1 or 2; no video is longer than 4 frames, and one is exactly that long.
All inputs are finite; a program needn't handle non-finite values.
Results may differ from a plain program's by a relative error of at most 0.0038.
Values may be sent and summed in bfloat16 or wider, within the bound.
A program may use at most 64 MiB of HBM per device.

v0:
```python
import jax
import jax.numpy as jnp
from jax import lax
from jax.sharding import PartitionSpec as P

GROUPS = 32


def from_behind(value, axis, steps):
    count = lax.axis_size(axis)
    leading, last = (max(0, -steps), min(count, count - steps))
    return lax.ppermute(value, axis, [(source, source + steps) for source in range(leading, last)])


def with_halo(shard, sides, width):
    for axis, dim in sides:
        size, length = (lax.axis_size(axis), shard.shape[dim])
        up = [(i, (i + 1) % size) for i in range(size - 1)]
        down = [(j, i) for i, j in up]
        last = lax.slice_in_dim(shard, length - width, length, axis=dim)
        leading = lax.slice_in_dim(shard, 0, width, axis=dim)
        before = lax.ppermute(last, axis, up)
        after = lax.ppermute(leading, axis, down)
        shard = jnp.concatenate([before, shard, after], axis=dim)
    return shard


def group_stats(values, groups):
    nf, nh, nw, nc = values.shape
    split = values.reshape(nf, nh, nw, groups, nc // groups)
    return (jnp.sum(split, axis=(1, 2, 4)), jnp.sum(split * split, axis=(1, 2, 4)))


def normalize(values, sum_one, sum_two, count, gain, shift, groups):
    mean = sum_one / count
    spread = sum_two / count - mean * mean
    scale = lax.rsqrt(spread + 1e-06)
    repeat = values.shape[3] // groups
    mean_c = jnp.repeat(mean, repeat, axis=1)[:, None, None, :]
    scale_c = jnp.repeat(scale, repeat, axis=1)[:, None, None, :]
    normed = (values - mean_c) * scale_c * gain + shift
    return jax.nn.silu(normed).astype(jnp.bfloat16)


def tap_sources(positions, offsets):
    steps = jnp.arange(3, dtype=jnp.int32)
    back = jnp.minimum(2 - steps[None, :], positions[:, None])
    return offsets[:, None] - back


def conv_frames(padded, wmat, sources):
    out_h = padded.shape[1] - 2
    out_w = padded.shape[2] - 2

    def one_frame(src):
        pieces = []
        for tap in range(3):
            frame = lax.dynamic_index_in_dim(padded, src[tap], 0, keepdims=False)
            for row_tap in range(3):
                for col_tap in range(3):
                    pieces.append(frame[row_tap : row_tap + out_h, col_tap : col_tap + out_w])
        columns = jnp.concatenate(pieces, axis=2).reshape(out_h * out_w, -1)
        result = jnp.dot(columns, wmat, preferred_element_type=jnp.float32)
        return result.reshape(out_h, out_w, -1)

    return lax.map(one_frame, sources)


def pad_columns(block):
    return jnp.pad(block, ((0, 0), (0, 0), (1, 1), (0, 0)))


def body(
    frames, video_pos, norm1_gain, norm1_shift, conv1_weight, norm2_gain, norm2_shift, conv2_weight
):
    local_t = frames.shape[0]
    chans = frames.shape[3]
    wmat_one = conv1_weight.reshape(27 * chans, chans)
    wmat_two = conv2_weight.reshape(27 * chans, chans)
    count = frames.shape[1] * lax.axis_size("rows") * frames.shape[2] * (chans // GROUPS)
    own_sources = tap_sources(video_pos, jnp.arange(local_t, dtype=jnp.int32) + 2)
    values = frames.astype(jnp.float32)
    sum_one, sum_two = group_stats(values, GROUPS)
    sum_one, sum_two = lax.psum((sum_one, sum_two), "rows")
    act_one = normalize(values, sum_one, sum_two, count, norm1_gain, norm1_shift, GROUPS)
    earlier = from_behind(act_one[local_t - 2 :], "tm", 1)
    extended = jnp.concatenate([earlier, act_one], axis=0)
    padded = pad_columns(with_halo(extended, (("rows", 1),), 1))
    middle = conv_frames(padded, wmat_one, own_sources)
    sum_one, sum_two = group_stats(middle, GROUPS)
    sum_one, sum_two = lax.psum((sum_one, sum_two), "rows")
    act_two = normalize(middle, sum_one, sum_two, count, norm2_gain, norm2_shift, GROUPS)
    earlier_two = from_behind(act_two[local_t - 2 :], "tm", 1)
    extended_two = jnp.concatenate([earlier_two, act_two], axis=0)
    padded_two = pad_columns(with_halo(extended_two, (("rows", 1),), 1))
    branch = conv_frames(padded_two, wmat_two, own_sources)
    return (frames.astype(jnp.float32) + branch).astype(jnp.bfloat16)


def solution(mesh):
    placed = (P("tm", "rows", None, None), P("tm"), P(), P(), P(), P(), P(), P())
    return jax.shard_map(
        body, mesh=mesh, in_specs=placed, out_specs=P("tm", "rows", None, None), check_vma=False
    )
```

profile of v0, /device:TPU:1, one launch (start us, length us, event | category | flops | bytes accessed | tf_op | source)
XLA Modules:
  0.0 614.0 jit_solution(974482957009493547)
XLA Ops:
  0.0 1.3 convert_reduce_fusion
  1.7 254.7 %all-reduce.3 = (f32[4,32]{1,0:T(4,128)S(1)}, f32[4,32]{1,0:T(4,128)S(1)}) all-reduce(f32[4,32]{1,0:T(4,128)S(1)} %reduce_sum.54, f32[4,32]{1,0:T(4,128)S(1)} %reduce_sum.51), channel_id=1, replica_groups=mesh['tm'=4,'rows'=128] {'rows'}, use_global_device_ids=true, to_apply=%region_5.6 | all-reduce | flops 256 | bytes 2048 | tf_op jit(solution)/shard_map/psum | solution.py:84
  256.8 1.5 fusion.23
  258.3 3.1 collective-permute-start
  261.4 3.3 collective-permute-done
  264.7 3.8 collective-permute-start.1
  268.5 5.2 collective-permute-start.2
  273.9 0.8 collective-permute-done.2
  275.4 36.1 %while.20 = (s32[]{:T(128)}, f32[4,8,64,128]{3,2,1,0:T(8,128)S(1)}, s32[4,3]{1,0:T(4,128)S(1)}, bf16[6,10,66,128]{3,2,1,0:T(8,128)(2,1)S(1)}, bf16[3456,128]{1,0...) while((s32[]{:T(128)}, f32[4,8,64,128]{3,2,1,0:T(8,128)S(1)}, s32[4,3]{1,0:T(4,128)S(1)}, ...), condition=%wide.region_7.8_spmd, body=%wide.region_6.7_spmd.sunk | while | flops 452984832 | bytes 12777727 | solution.py:66
  275.5 0.7 fusion.41
  283.4 1.1 fusion.42
  284.5 0.7 fusion.41
  292.4 1.1 fusion.42
  293.5 0.7 fusion.41
  301.4 1.1 fusion.42
  302.5 0.7 fusion.41
  310.4 1.1 fusion.42
  312.0 246.5 %all-reduce.2 = (f32[4,32]{1,0:T(4,128)S(1)}, f32[4,32]{1,0:T(4,128)S(1)}) all-reduce(f32[4,32]{1,0:T(4,128)S(1)} %reduce_sum.75, f32[4,32]{1,0:T(4,128)S(1)} %reduce_sum.72), channel_id=1, replica_groups=mesh['tm'=4,'rows'=128] {'rows'}, use_global_device_ids=true, to_apply=%region_13.14 | all-reduce | flops 256 | bytes 2048 | tf_op jit(solution)/shard_map/psum | solution.py:91
  559.4 4.1 collective-permute-start.3
  563.5 4.8 collective-permute-done.3
  568.3 1.9 collective-permute-start.4
  570.3 3.0 collective-permute-start.5
  573.2 3.0 collective-permute-done.5
  576.9 36.1 %while.21 = (s32[]{:T(128)}, f32[4,8,64,128]{3,2,1,0:T(8,128)S(1)}, s32[4,3]{1,0:T(4,128)S(1)}, bf16[6,10,66,128]{3,2,1,0:T(8,128)(2,1)S(1)}, bf16[3456,128]{1,0...) while((s32[]{:T(128)}, f32[4,8,64,128]{3,2,1,0:T(8,128)S(1)}, s32[4,3]{1,0:T(4,128)S(1)}, ...), condition=%wide.region_15.16_spmd, body=%wide.region_14.15_spmd.sunk | while | flops 452984832 | bytes 16316699 | solution.py:66
  576.9 0.7 fusion.45
  584.8 1.1 fusion.46
  586.0 0.7 fusion.45
  593.9 1.1 fusion.46
  602.9 1.1 fusion.46
  604.0 0.7 fusion.45
  611.9 1.1 fusion.46
  613.0 1.0 fusion.25
  (284 shorter events, 15.4 us)
Async XLA Ops:
  0.0 273.8 %copy-start.3 = (s32[4]{0:T(128)S(1)}, s32[4]{0:T(128)}, u32[]{:S(2)}) copy-start(s32[4]{0:T(128)} %param.13) | copy-start | bytes 52
  0.0 275.4 %copy-start.4 = (bf16[3,3,3,128,128]{4,3,2,1,0:T(8,128)(2,1)S(1)}, bf16[3,3,3,128,128]{4,3,2,1,0:T(8,128)(2,1)}, u32[]{:S(2)}) copy-start(bf16[3,3,3,128,128]{4,3,2,1,0:T(8,128)(2,1)} %param.16) | copy-start | bytes 2654212
  258.3 6.4 %collective-permute-start = (bf16[2,8,64,128]{3,2,1,0:T(8,128)(2,1)S(1)}, bf16[2,8,64,128]{3,2,1,0:T(8,128)(2,1)S(1)}, u32[]{:S(2)}, u32[]{:S(2)}) collective-permute-start(bf16[2,8,64,128]{3,2,1,0:T(8,128)(2,1)S(1)} %slice.264), channel_id=1, source_target_pairs={{0,128},{128,256},{256,384},{1,129},{129,257},{257,385},{2,130},{1... | collective-permute-start | bytes 786440 | tf_op jit(solution)/shard_map/ppermute | solution.py:12
  264.7 9.2 %collective-permute-start.1 = (bf16[6,1,64,128]{3,2,1,0:T(8,128)(2,1)S(1)}, bf16[6,1,64,128]{3,2,1,0:T(8,128)(2,1)S(1)}, u32[]{:S(2)}, u32[]{:S(2)}) collective-permute-start(bf16[6,1,64,128]{3,2,1,0:T(8,128)(2,1)S(1)} %get-tuple-element.103), channel_id=1, source_target_pairs={{0,1},{1,2},{2,3},{3,4},{4,5},{5,6},{6,7},{7,8},{8,9},{9,10},{10,1... | collective-permute-start | bytes 294920 | tf_op jit(solution)/shard_map/ppermute | solution.py:22
  268.5 6.2 %collective-permute-start.2 = (bf16[6,1,64,128]{3,2,1,0:T(8,128)(2,1)S(1)}, bf16[6,1,64,128]{3,2,1,0:T(8,128)(2,1)S(1)}, u32[]{:S(2)}, u32[]{:S(2)}) collective-permute-start(bf16[6,1,64,128]{3,2,1,0:T(8,128)(2,1)S(1)} %get-tuple-element.104), channel_id=1, source_target_pairs={{1,0},{2,1},{3,2},{4,3},{5,4},{6,5},{7,6},{8,7},{9,8},{10,9},{11,1... | collective-permute-start | bytes 294920 | tf_op jit(solution)/shard_map/ppermute | solution.py:23
  275.4 283.6 %copy-start.1 = (f32[128]{0:T(128)S(1)}, f32[128]{0:T(128)}, u32[]{:S(2)}) copy-start(f32[128]{0:T(128)} %param.18) | copy-start | bytes 1540
  275.4 283.6 %copy-start.2 = (f32[128]{0:T(128)S(1)}, f32[128]{0:T(128)}, u32[]{:S(2)}) copy-start(f32[128]{0:T(128)} %param.17) | copy-start | bytes 1540
  559.4 8.9 %collective-permute-start.3 = (bf16[2,8,64,128]{3,2,1,0:T(8,128)(2,1)S(1)}, bf16[2,8,64,128]{3,2,1,0:T(8,128)(2,1)S(1)}, u32[]{:S(2)}, u32[]{:S(2)}) collective-permute-start(bf16[2,8,64,128]{3,2,1,0:T(8,128)(2,1)S(1)} %slice.265), channel_id=1, source_target_pairs={{0,128},{128,256},{256,384},{1,129},{129,257},{257,385},{2,130},{1... | collective-permute-start | bytes 786440 | tf_op jit(solution)/shard_map/ppermute | solution.py:12
  568.3 4.9 collective-permute-start.4
  570.3 5.9 collective-permute-start.5
  576.9 36.2 %copy-start = (bf16[4,8,64,128]{3,2,1,0:T(8,128)(2,1)S(1)}, bf16[4,8,64,128]{3,2,1,0:T(8,128)(2,1)}, u32[]{:S(2)}) copy-start(bf16[4,8,64,128]{3,2,1,0:T(8,128)(2,1)} %param.12) | copy-start | bytes 1572868
  583.3 1.5 copy-start.5
  592.3 1.5 copy-start.5
  601.4 1.5 copy-start.5
  610.4 1.5 copy-start.5
where the time goes:
time: 623 us; the launch traced here: 614 us
  blocking collectives  501 us (80%)
  loops' own time  47 us (8%)
  starting transfers between devices  21.2 us (3%)
  local copies, waits for them, and re-layouts  18 us (3%)
  waiting for transfers between devices  11.9 us (2%)
  matrix products  8.65 us (1%)
    psum x2, blocking collectives, body(): sum_one, sum_two = lax.psum((sum_one, sum_two), 'rows')  501 us
    another operation x2, loops' own time, conv_frames(): return lax.map(one_frame, sources)  47 us
  transfers between devices with their start and end apart: 6, of which 4 were waited for; matrix products, arithmetic and copies ran while one was open for 0% of the time, Pallas kernels for 0%

commit v1 on v0

v1 whole, which is shorter than its diff:
```python
import functools

import jax
import jax.numpy as jnp
from jax import lax
from jax.experimental import pallas as pl
from jax.experimental.pallas import tpu as pltpu
from jax.sharding import PartitionSpec as P

GROUP = 4
EPS = 1e-06
MESH = pl.DeviceIdType.MESH


def near_size(rows):
    size = 1
    while size * size < rows:
        size *= 2
    return size


def kernel(
    nt,
    nr,
    frames,
    video_pos,
    gain1,
    shift1,
    weight1,
    gain2,
    shift2,
    weight2,
    out,
    ext,
    ext2,
    own2,
    mid,
    act,
    pad,
    wraw,
    wpair,
    params,
    pos,
    affine,
    stat,
    part,
    near,
    far,
    prev,
    result,
    load_sem,
    out_sem,
    send_sem,
    recv_sem,
):
    nf, hr, wc, ch = frames.shape
    pairs = hr // 2
    near_n = near.shape[1]
    far_n = far.shape[1]
    count = float(nr * hr * wc * GROUP)
    t = lax.axis_index("tm")
    r = lax.axis_index("rows")
    in_near = lax.rem(r, near_n)
    in_far = lax.div(r, near_n)
    above = lax.rem(r + nr - 1, nr)
    below = lax.rem(r + 1, nr)
    after = lax.rem(t + 1, nt)
    before = lax.rem(t + nt - 1, nt)

    def near_peer(step):
        return in_far * near_n + lax.rem(in_near + step, near_n)

    def far_peer(step):
        return lax.rem(in_far + step, far_n) * near_n + in_near

    loads = [
        pltpu.make_async_copy(frames, ext.at[2 : 2 + nf, 1 : 1 + hr], load_sem.at[0]),
        pltpu.make_async_copy(weight1, wraw.at[0], load_sem.at[1]),
        pltpu.make_async_copy(weight2, wraw.at[1], load_sem.at[2]),
        pltpu.make_async_copy(video_pos, pos, load_sem.at[3]),
        pltpu.make_async_copy(gain1, params.at[0], load_sem.at[4]),
        pltpu.make_async_copy(shift1, params.at[1], load_sem.at[5]),
        pltpu.make_async_copy(gain2, params.at[2], load_sem.at[6]),
        pltpu.make_async_copy(shift2, params.at[3], load_sem.at[7]),
    ]
    for load in loads:
        load.start()

    barrier = pltpu.get_barrier_semaphore()

    def greet(tt, rr):
        pl.semaphore_signal(barrier, inc=1, device_id=(tt, rr), device_id_type=MESH)

    @pl.loop(1, near_n)
    def _(step):
        greet(t, near_peer(step))

    @pl.loop(1, far_n)
    def _(step):
        greet(t, far_peer(step))

    greet(t, above)
    greet(t, below)
    greet(before, r)
    greet(before, above)
    greet(before, below)

    def send(src, dst, which, tt, rr):
        return pltpu.make_async_remote_copy(
            src_ref=src,
            dst_ref=dst,
            send_sem=send_sem.at[which],
            recv_sem=recv_sem.at[which],
            device_id=(tt, rr),
            device_id_type=MESH,
        )

    def sum_start(phase):
        @pl.loop(1, near_n)
        def _(step):
            send(
                stat.at[phase], near.at[phase, in_near], 2 * phase, t, near_peer(step)
            ).start()

        near[phase, in_near] = stat[phase]

    def wait_many(ref, sem):
        pltpu.make_async_copy(ref, ref, sem).wait()

    def sum_middle(phase):
        wait_many(near.at[phase, 0 : near_n - 1], recv_sem.at[2 * phase])
        total = near[phase, 0]
        for i in range(1, near_n):
            total = total + near[phase, i]
        part[phase] = total
        far[phase, in_far] = total

        @pl.loop(1, far_n)
        def _(step):
            send(
                part.at[phase], far.at[phase, in_far], 2 * phase + 1, t, far_peer(step)
            ).start()

    def sum_end(phase):
        wait_many(far.at[phase, 0 : far_n - 1], recv_sem.at[2 * phase + 1])
        total = far[phase, 0]
        for i in range(1, far_n):
            total = total + far[phase, i]
        lane = lax.broadcasted_iota(jnp.int32, total.shape, 1)
        for width in (1, 2):
            up = pltpu.roll(total, width, 1)
            down = pltpu.roll(total, ch - width, 1)
            total = total + jnp.where(lax.rem(lax.div(lane, width), 2) == 0, down, up)
        stat[2 + phase] = total

    def sum_drain(phase):
        wait_many(near.at[phase, 0 : near_n - 1], send_sem.at[2 * phase])
        wait_many(far.at[phase, 0 : far_n - 1], send_sem.at[2 * phase + 1])

    def set_affine(phase, total, first, number, at):
        mean = total[first : first + number] / count
        spread = total[nf + first : nf + first + number] / count - mean * mean
        scale = lax.rsqrt(spread + EPS) * params[2 * phase]
        affine[phase, 0, at : at + number] = scale
        affine[phase, 1, at : at + number] = params[2 * phase + 1] - mean * scale

    def fill_weights(layer):
        wp = wpair.at[layer]
        zeros = jnp.zeros((3 * ch, ch), wp.dtype)
        for k in range(3):
            for u in range(4):
                at = (4 * k + u) * 3 * ch
                for par in range(2):
                    i = u - par
                    block = wraw[layer, (3 * k + i) * 3 * ch : (3 * k + i + 1) * 3 * ch] if 0 <= i < 3 else zeros
                    wp[at : at + 3 * ch, par * ch : (par + 1) * ch] = block

    row_ok = (
        jnp.where(r > 0, 1.0, 0.0).astype(jnp.float32),
        jnp.where(r < nr - 1, 1.0, 0.0).astype(jnp.float32),
    )

    def norm_row(x, phase, s, row, slot):
        y = x * affine[phase, 0, pl.ds(s, 1)] + affine[phase, 1, pl.ds(s, 1)]
        a = y * (0.5 * jnp.tanh(0.5 * y) + 0.5)
        if row == 0:
            a = a * row_ok[0]
        if row == hr + 1:
            a = a * row_ok[1]
        pad[slot, 8 : 8 + wc] = a
        lo = (row % 2) * 3 * ch
        act[s, row // 2, :, lo : lo + ch] = pad[slot, 7 : 7 + wc].astype(act.dtype)
        act[s, row // 2, :, lo + ch : lo + 2 * ch] = a.astype(act.dtype)
        act[s, row // 2, :, lo + 2 * ch : lo + 3 * ch] = pad[slot, 9 : 9 + wc].astype(act.dtype)

    def norm_frames(phase, first, last):
        @pl.loop(first, last)
        def _(s):
            for row in range(hr + 2):
                if phase == 0:
                    x = ext[s, row].astype(jnp.float32)
                elif first < 2 or row in (0, hr + 1):
                    x = ext2[s, row].astype(jnp.float32)
                else:
                    q = row - 1
                    x = mid[s - 2, q // 2, :, (q % 2) * ch : (q % 2 + 1) * ch]
                norm_row(x, phase, s, row, row)

    def conv(layer, f):
        pieces = []
        for k in range(3):
            s = f + 2 - jnp.minimum(2 - k, pos[f])
            for half in range(2):
                pieces.append(act[s, half : half + pairs].reshape(pairs * wc, 6 * ch))
        lhs = jnp.concatenate(pieces, axis=1)
        total = jnp.dot(lhs, wpair[layer], preferred_element_type=jnp.float32)
        return total.reshape(pairs, wc, 2 * ch)

    def fold(x):
        while x.shape[0] > 1:
            half = x.shape[0] // 2
            x = x[:half] + x[half:]
        return x

    def column_sums(x):
        return jnp.sum(x, axis=0, keepdims=True)

    loads[0].wait()
    @pl.loop(0, nf)
    def _(f):
        one = jnp.zeros((8, ch), jnp.float32)
        two = jnp.zeros((8, ch), jnp.float32)
        for row in range(1, hr + 1):
            x = ext[f + 2, row].astype(jnp.float32).reshape(wc // 8, 8, ch)
            one = one + jnp.sum(x, axis=0)
            two = two + jnp.sum(x * x, axis=0)
        stat[0, pl.ds(f, 1)] = column_sums(one)
        stat[0, pl.ds(f + nf, 1)] = column_sums(two)

    pl.semaphore_wait(barrier, near_n + far_n - 2 + 5)
    sum_start(0)

    halos = [
        send(frames.at[:, hr - 1], ext.at[2 : 2 + nf, 0], 4, t, below),
        send(frames.at[:, 0], ext.at[2 : 2 + nf, hr + 1], 5, t, above),
        send(frames.at[nf - 2 : nf, hr - 1], ext.at[0:2, 0], 6, after, below),
        send(frames.at[nf - 2 : nf, 0], ext.at[0:2, hr + 1], 7, after, above),
        send(frames.at[nf - 2 : nf], ext.at[0:2, 1 : 1 + hr], 8, after, r),
    ]
    for halo in halos:
        halo.start()

    loads[1].wait()
    fill_weights(0)
    for slot in range(hr + 2):
        pad[slot, 0:8] = jnp.zeros((8, ch), jnp.float32)
        pad[slot, 8 + wc : 16 + wc] = jnp.zeros((8, ch), jnp.float32)
    sum_middle(0)
    loads[2].wait()
    fill_weights(1)
    for load in loads[3:]:
        load.wait()
    sum_end(0)
    ahead = send(stat.at[2], prev.at[0], 9, after, r)
    ahead.start()
    set_affine(0, stat[2], 0, nf, 2)
    halos[0].wait_recv()
    halos[1].wait_recv()
    norm_frames(0, 2, 2 + nf)

    def conv_one(f):
        total = conv(0, f)
        mid[f] = total
        one = jnp.sum(total.reshape(pairs * wc // 8, 8, 2 * ch), axis=0)
        two = jnp.sum((total * total).reshape(pairs * wc // 8, 8, 2 * ch), axis=0)
        one = column_sums(one[:, :ch] + one[:, ch:])
        two = column_sums(two[:, :ch] + two[:, ch:])
        stat[1, f : f + 1] = one
        stat[1, f + nf : f + nf + 1] = two
        for row in range(hr):
            if f >= nf - 2 or row in (0, hr - 1):
                own2[f, row] = total[row // 2, :, (row % 2) * ch : (row % 2 + 1) * ch].astype(own2.dtype)

    conv_one(nf - 1)
    conv_one(nf - 2)
    halos2 = [
        send(own2.at[nf - 2 : nf, hr - 1], ext2.at[0:2, 0], 10, after, below),
        send(own2.at[nf - 2 : nf, 0], ext2.at[0:2, hr + 1], 11, after, above),
        send(own2.at[nf - 2 : nf], ext2.at[0:2, 1 : 1 + hr], 12, after, r),
    ]
    for halo in halos2:
        halo.start()

    ahead.wait_recv()
    set_affine(0, prev[0], nf - 2, 2, 0)
    for halo in halos[2:]:
        halo.wait_recv()
    norm_frames(0, 0, 2)
    conv_one(0)
    conv_one(1)
    sum_start(1)
    edges2 = [
        send(own2.at[:, hr - 1], ext2.at[2 : 2 + nf, 0], 13, t, below),
        send(own2.at[:, 0], ext2.at[2 : 2 + nf, hr + 1], 14, t, above),
    ]
    for edge in edges2:
        edge.start()
    sum_middle(1)
    sum_end(1)
    ahead2 = send(stat.at[3], prev.at[1], 15, after, r)
    ahead2.start()
    set_affine(1, stat[3], 0, nf, 2)
    for edge in edges2:
        edge.wait_recv()
    norm_frames(1, 2, 2 + nf)

    def conv_two(f):
        total = conv(1, f)
        for row in range(hr):
            piece = total[row // 2, :, (row % 2) * ch : (row % 2 + 1) * ch]
            kept = ext[f + 2, row + 1].astype(jnp.float32)
            result[f, row] = (kept + piece).astype(result.dtype)
        copy = pltpu.make_async_copy(result.at[f], out.at[f], out_sem.at[f])
        copy.start()
        return copy

    copies = [conv_two(nf - 1), conv_two(nf - 2)]
    ahead2.wait_recv()
    set_affine(1, prev[1], nf - 2, 2, 0)
    for halo in halos2:
        halo.wait_recv()
    norm_frames(1, 0, 2)
    copies += [conv_two(0), conv_two(1)]
    for sent in halos + halos2 + edges2 + [ahead, ahead2]:
        sent.wait_send()
    sum_drain(0)
    sum_drain(1)
    for copy in copies:
        copy.wait()


def body(frames, video_pos, gain1, shift1, weight1, gain2, shift2, weight2):
    nt = lax.axis_size("tm")
    nr = lax.axis_size("rows")
    nf, hr, wc, ch = frames.shape
    near_n = near_size(nr)
    far_n = nr // near_n
    bf, f32 = jnp.bfloat16, jnp.float32
    hbm = pl.BlockSpec(memory_space=pl.ANY)
    call = pl.pallas_call(
        functools.partial(kernel, nt, nr),
        out_shape=jax.ShapeDtypeStruct(frames.shape, frames.dtype),
        in_specs=[hbm] * 8,
        out_specs=hbm,
        scratch_shapes=[
            pltpu.VMEM((nf + 2, hr + 2, wc, ch), bf),
            pltpu.VMEM((nf + 2, hr + 2, wc, ch), bf),
            pltpu.VMEM((nf, hr, wc, ch), bf),
            pltpu.VMEM((nf, hr // 2, wc, 2 * ch), f32),
            pltpu.VMEM((nf + 2, hr // 2 + 1, wc, 6 * ch), bf),
            pltpu.VMEM((hr + 2, wc + 16, ch), f32),
            pltpu.VMEM((2, 27 * ch, ch), bf),
            pltpu.VMEM((2, 36 * ch, 2 * ch), bf),
            pltpu.VMEM((4, 1, ch), f32),
            pltpu.SMEM((nf,), jnp.int32),
            pltpu.VMEM((2, 2, 8, ch), f32),
            pltpu.VMEM((4, 2 * nf, ch), f32),
            pltpu.VMEM((2, 2 * nf, ch), f32),
            pltpu.VMEM((2, near_n, 2 * nf, ch), f32),
            pltpu.VMEM((2, far_n, 2 * nf, ch), f32),
            pltpu.VMEM((2, 2 * nf, ch), f32),
            pltpu.VMEM((nf, hr, wc, ch), bf),
            pltpu.SemaphoreType.DMA((8,)),
            pltpu.SemaphoreType.DMA((nf,)),
            pltpu.SemaphoreType.DMA((16,)),
            pltpu.SemaphoreType.DMA((16,)),
        ],
        compiler_params=pltpu.CompilerParams(
            collective_id=0, has_side_effects=True, vmem_limit_bytes=48 * 1024 * 1024
        ),
        name="encoder_block",
    )
    return call(
        frames,
        video_pos,
        gain1.reshape(1, ch),
        shift1.reshape(1, ch),
        weight1.reshape(27 * ch, ch),
        gain2.reshape(1, ch),
        shift2.reshape(1, ch),
        weight2.reshape(27 * ch, ch),
    )


def solution(mesh):
    placed = (P("tm", "rows", None, None), P("tm"), P(), P(), P(), P(), P(), P())
    return jax.shard_map(
        body, mesh=mesh, in_specs=placed, out_specs=P("tm", "rows", None, None), check_vma=False
    )
```

time: 623 us -> 53 us (0.09); the launches traced: 614 us -> 52.7 us
  blocking collectives: 501 us -> 0 us
  Pallas kernels: 0 us -> 47.8 us
  loops' own time: 47 us -> 0 us
  starting transfers between devices: 21.2 us -> 0 us
  local copies, waits for them, and re-layouts: 18 us -> 4.87 us
  waiting for transfers between devices: 11.9 us -> 0 us
  matrix products: 8.65 us -> 0 us
    psum x2 -> x0, blocking collectives: 501 us -> none  [body(): sum_one, sum_two = lax.psum((sum_one, sum_two), 'rows')]
    pallas_call x0 -> x1, Pallas kernels: none -> 47.8 us  [body(): call(frames, video_pos, gain1.reshape(1, ch), shift1.reshape(1, ch), weig...]
    another operation x2 -> x0, loops' own time: 47 us -> none  [conv_frames(): return lax.map(one_frame, sources)]
    ppermute x6 -> x0, starting transfers between devices: 21.2 us -> none  [the longest x2 8.21 us: with_halo(): after = lax.ppermute(leading, axis, down)]
    ppermute x6 -> x0, waiting for transfers between devices: 11.9 us -> none  [the longest x2 8.07 us: from_behind(): lax.ppermute(value, axis, [(source, source + steps) for source in range(l...]
    while x216 -> x0, local copies, waits for them, and re-layouts: 10.2 us -> none
    dot_general x8 -> x0, matrix products: 8.65 us -> none  [one_frame(): result = jnp.dot(columns, wmat, preferred_element_type=jnp.float32)]
  transfers between devices with their start and end apart: 6 -> 0, of which waited for: 4 -> 0; matrix products, arithmetic and copies ran while one was open for 0% -> 0% of each run, Pallas kernels for 0% -> 0%
where the time goes in v1:
time: 53 us; the launch traced here: 52.7 us
  Pallas kernels  47.8 us (90%)
  local copies, waits for them, and re-layouts  4.87 us (9%)
    pallas_call x1, Pallas kernels, body(): call(frames, video_pos, gain1.reshape(1, ch), shift1.reshape(1, ch), weig...  47.8 us
    unnamed x17, local copies, waits for them, and re-layouts  4.87 us

profile of v1, /device:TPU:1, one launch (start us, length us, event | category | flops | bytes accessed | tf_op | source)
XLA Modules:
  0.0 52.7 jit_solution(4539950241977488394)
XLA Ops:
  0.0 0.0 copy-start.6
  0.0 0.0 copy-start.7
  0.0 0.0 copy-start.3
  0.0 0.0 copy-start.4
  0.0 0.0 copy-start.5
  0.0 0.6 %copy-done.6 = f32[128]{0:T(128)S(1)} copy-done((f32[128]{0:T(128)S(1)}, f32[128]{0:T(128)}, u32[]{:S(2)}) %copy-start.6) | copy-done | bytes 536
  0.7 0.0 copy-done.7
  0.7 0.0 copy-done.3
  0.7 0.0 copy-done.4
  0.7 0.0 copy-done.5
  0.7 0.0 copy-start
  0.7 1.2 %copy-done = bf16[3,3,3,128,128]{4,3,2,1,0:T(8,128)(2,1)S(1)} copy-done((bf16[3,3,3,128,128]{4,3,2,1,0:T(8,128)(2,1)S(1)}, bf16[3,3,3,128,128]{4,3,2,1,0:T(8,128)(2,1)}, u32[]{:S(2)}) %copy-start) | copy-done | bytes 884760
  1.9 0.0 copy-start.1
  1.9 1.2 %copy-done.1 = bf16[3,3,3,128,128]{4,3,2,1,0:T(8,128)(2,1)S(1)} copy-done((bf16[3,3,3,128,128]{4,3,2,1,0:T(8,128)(2,1)S(1)}, bf16[3,3,3,128,128]{4,3,2,1,0:T(8,128)(2,1)}, u32[]{:S(2)}) %copy-start.1) | copy-done | bytes 884760
  3.1 0.0 copy-start.2
  3.1 1.0 %copy-done.2 = bf16[4,8,64,128]{3,2,1,0:T(8,128)(2,1)S(1)} copy-done((bf16[4,8,64,128]{3,2,1,0:T(8,128)(2,1)S(1)}, bf16[4,8,64,128]{3,2,1,0:T(8,128)(2,1)}, u32[]{:S(2)}) %copy-start.2) | copy-done | bytes 524312
  4.1 47.8 %encoder_block.1 = bf16[4,8,64,128]{3,2,1,0:T(8,128)(2,1)S(1)} custom-call(bf16[4,8,64,128]{3,2,1,0:T(8,128)(2,1)S(1)} %copy-done.2, s32[4]{0:T(128)S(1)} %copy-done.3, f32[1,128]{1,0:T(1,128)S(1)} %bitcast.8, f32[1,128]{1,0:T(1,128)S(1)} %bitcast.9, bf16[3456,128]{1,0:T(8,128)(2,1)S(1)} %bitcast.6, f32[1,128]{1,0:T(1,128)S(1)} %bitcast.10, ...), custom_call_target="tpu_custom_call" | custom-call | tf_op jit(solution)/shard_map/encoder_block/pallas_call | solution.py:383
  51.9 0.8 %copy.10 = bf16[4,8,64,128]{3,2,1,0:T(8,128)(2,1)} copy(bf16[4,8,64,128]{3,2,1,0:T(8,128)(2,1)S(1)} %encoder_block.1) | data formatting | bytes 1048576
Async XLA Ops:
  0.0 0.7 %copy-start.6 = (f32[128]{0:T(128)S(1)}, f32[128]{0:T(128)}, u32[]{:S(2)}) copy-start(f32[128]{0:T(128)} %param.13) | copy-start | bytes 1540
  0.0 0.7 %copy-start.7 = (f32[128]{0:T(128)S(1)}, f32[128]{0:T(128)}, u32[]{:S(2)}) copy-start(f32[128]{0:T(128)} %param.14) | copy-start | bytes 1540
  0.0 0.7 %copy-start.3 = (s32[4]{0:T(128)S(1)}, s32[4]{0:T(128)}, u32[]{:S(2)}) copy-start(s32[4]{0:T(128)} %video_pos.1) | copy-start | bytes 52
  0.0 0.7 %copy-start.4 = (f32[128]{0:T(128)S(1)}, f32[128]{0:T(128)}, u32[]{:S(2)}) copy-start(f32[128]{0:T(128)} %param.10) | copy-start | bytes 1540
  0.0 0.7 %copy-start.5 = (f32[128]{0:T(128)S(1)}, f32[128]{0:T(128)}, u32[]{:S(2)}) copy-start(f32[128]{0:T(128)} %param.11) | copy-start | bytes 1540
  0.7 1.2 %copy-start = (bf16[3,3,3,128,128]{4,3,2,1,0:T(8,128)(2,1)S(1)}, bf16[3,3,3,128,128]{4,3,2,1,0:T(8,128)(2,1)}, u32[]{:S(2)}) copy-start(bf16[3,3,3,128,128]{4,3,2,1,0:T(8,128)(2,1)} %param.12) | copy-start | bytes 2654212
  1.9 1.2 %copy-start.1 = (bf16[3,3,3,128,128]{4,3,2,1,0:T(8,128)(2,1)S(1)}, bf16[3,3,3,128,128]{4,3,2,1,0:T(8,128)(2,1)}, u32[]{:S(2)}) copy-start(bf16[3,3,3,128,128]{4,3,2,1,0:T(8,128)(2,1)} %param.15) | copy-start | bytes 2654212
  3.1 1.0 %copy-start.2 = (bf16[4,8,64,128]{3,2,1,0:T(8,128)(2,1)S(1)}, bf16[4,8,64,128]{3,2,1,0:T(8,128)(2,1)}, u32[]{:S(2)}) copy-start(bf16[4,8,64,128]{3,2,1,0:T(8,128)(2,1)} %frames.1) | copy-start | bytes 1572868

commit v2 on v1

v2 whole, which is shorter than its diff:
```python
import functools

import jax
import jax.numpy as jnp
from jax import lax
from jax.experimental import pallas as pl
from jax.experimental.pallas import tpu as pltpu
from jax.sharding import PartitionSpec as P

GROUP = 4
EPS = 1e-06
MESH = pl.DeviceIdType.MESH


def near_size(rows):
    size = 1
    while size * size < rows:
        size *= 2
    return size


def kernel(
    nt,
    nr,
    frames,
    video_pos,
    gain1,
    shift1,
    weight1,
    gain2,
    shift2,
    weight2,
    out,
    ext,
    ext2,
    own2,
    mid,
    acc,
    act,
    pad,
    wraw,
    wpair,
    params,
    pos,
    affine,
    stat,
    packed,
    part,
    near,
    far,
    prev,
    load_sem,
    send_sem,
    recv_sem,
):
    nf, hr, wc, ch = frames.shape
    pairs = hr // 2
    near_n = near.shape[1]
    far_n = far.shape[1]
    count = float(nr * hr * wc * GROUP)
    t = lax.axis_index("tm")
    r = lax.axis_index("rows")
    in_near = lax.rem(r, near_n)
    in_far = lax.div(r, near_n)
    above = lax.rem(r + nr - 1, nr)
    below = lax.rem(r + 1, nr)
    after = lax.rem(t + 1, nt)
    before = lax.rem(t + nt - 1, nt)

    def near_peer(step):
        return in_far * near_n + lax.rem(in_near + step, near_n)

    def far_peer(step):
        return lax.rem(in_far + step, far_n) * near_n + in_near

    loads = [
        pltpu.make_async_copy(frames, ext.at[2 : 2 + nf, 1 : 1 + hr], load_sem.at[0]),
        pltpu.make_async_copy(weight1, wraw.at[0], load_sem.at[1]),
        pltpu.make_async_copy(weight2, wraw.at[1], load_sem.at[2]),
        pltpu.make_async_copy(video_pos, pos, load_sem.at[3]),
        pltpu.make_async_copy(gain1, params.at[0], load_sem.at[4]),
        pltpu.make_async_copy(shift1, params.at[1], load_sem.at[5]),
        pltpu.make_async_copy(gain2, params.at[2], load_sem.at[6]),
        pltpu.make_async_copy(shift2, params.at[3], load_sem.at[7]),
    ]
    for load in loads:
        load.start()

    barrier = pltpu.get_barrier_semaphore()

    def greet(tt, rr):
        pl.semaphore_signal(barrier, inc=1, device_id=(tt, rr), device_id_type=MESH)

    @pl.loop(1, near_n)
    def _(step):
        greet(t, near_peer(step))

    @pl.loop(1, far_n)
    def _(step):
        greet(t, far_peer(step))

    @pl.loop(0, far_n)
    def _(step):
        greet(before, far_peer(step))

    greet(t, above)
    greet(t, below)
    greet(before, above)
    greet(before, below)

    def send(src, dst, which, tt, rr):
        return pltpu.make_async_remote_copy(
            src_ref=src,
            dst_ref=dst,
            send_sem=send_sem.at[which],
            recv_sem=recv_sem.at[which],
            device_id=(tt, rr),
            device_id_type=MESH,
        )

    lane = lax.broadcasted_iota(jnp.int32, (8, ch), 1)
    own_lane = lax.rem(lane, GROUP) == lax.rem(lax.broadcasted_iota(jnp.int32, (8, ch), 0), GROUP)

    def group_sums(x):
        for width in (1, 2):
            up = pltpu.roll(x, width, 1)
            down = pltpu.roll(x, ch - width, 1)
            x = x + jnp.where(lax.rem(lax.div(lane, width), 2) == 0, down, up)
        return x

    def sum_start(phase):
        own = jnp.where(own_lane, group_sums(stat[phase]), 0.0)
        one = jnp.sum(own[:nf], axis=0, keepdims=True)
        two = jnp.sum(own[nf:], axis=0, keepdims=True)
        packed[phase] = jnp.concatenate([one, two], axis=0)
        near[phase, in_near] = packed[phase]

        @pl.loop(1, near_n)
        def _(step):
            send(
                packed.at[phase], near.at[phase, in_near], 3 * phase, t, near_peer(step)
            ).start()

    def wait_many(ref, sem):
        pltpu.make_async_copy(ref, ref, sem).wait()

    def sum_middle(phase):
        wait_many(near.at[phase, 0 : near_n - 1], recv_sem.at[3 * phase])
        total = jnp.sum(near[phase], axis=0)
        part[phase] = total
        far[phase, in_far] = total

        @pl.loop(1, far_n)
        def _(step):
            send(
                part.at[phase], far.at[phase, in_far], 3 * phase + 1, t, far_peer(step)
            ).start()

        @pl.loop(0, far_n)
        def _(step):
            send(
                part.at[phase], prev.at[phase, in_far], 3 * phase + 2, after, far_peer(step)
            ).start()

    def sum_drain(phase):
        wait_many(near.at[phase, 0 : near_n - 1], send_sem.at[3 * phase])
        wait_many(far.at[phase, 0 : far_n - 1], send_sem.at[3 * phase + 1])
        wait_many(prev.at[phase], send_sem.at[3 * phase + 2])

    def set_affine(phase, total, at):
        sums = [
            group_sums(jnp.where(own_lane, jnp.broadcast_to(total[i : i + 1], (8, ch)), 0.0))
            for i in range(2)
        ]
        mean = sums[0] / count
        spread = sums[1] / count - mean * mean
        scale = lax.rsqrt(spread + EPS) * params[2 * phase]
        affine[phase, at, 0] = scale
        affine[phase, at, 1] = params[2 * phase + 1] - mean * scale

    def own_affine(phase):
        wait_many(far.at[phase, 0 : far_n - 1], recv_sem.at[3 * phase + 1])
        set_affine(phase, jnp.sum(far[phase], axis=0), 1)

    def prev_affine(phase):
        wait_many(prev.at[phase], recv_sem.at[3 * phase + 2])
        set_affine(phase, jnp.sum(prev[phase], axis=0), 0)

    def fill_weights(layer):
        zeros = jnp.zeros((3 * ch, ch), wpair.dtype)
        for k in range(3):
            for i in range(3):
                tap = wraw[layer, (3 * k + i) * 3 * ch : (3 * k + i + 1) * 3 * ch]
                for par in range(2):
                    u = i + par
                    wpair[layer, k, u * 3 * ch : (u + 1) * 3 * ch, par * ch : (par + 1) * ch] = tap
            wpair[layer, k, 9 * ch : 12 * ch, 0:ch] = zeros
            wpair[layer, k, 0 : 3 * ch, ch : 2 * ch] = zeros

    row_ok = (
        jnp.where(r > 0, 1.0, 0.0).astype(jnp.float32),
        jnp.where(r < nr - 1, 1.0, 0.0).astype(jnp.float32),
    )

    def norm_row(x, phase, s, row, own):
        f = s - 2 if own else s + nf - 2
        slot = row
        y = x * affine[phase, int(own), 0, pl.ds(f, 1)] + affine[phase, int(own), 1, pl.ds(f, 1)]
        a = y * (0.5 * jnp.tanh(0.5 * y) + 0.5)
        if row == 0:
            a = a * row_ok[0]
        if row == hr + 1:
            a = a * row_ok[1]
        pad[slot, 8 : 8 + wc] = a
        lo = (row % 2) * 3 * ch
        act[s, row // 2, :, lo : lo + ch] = pad[slot, 7 : 7 + wc].astype(act.dtype)
        act[s, row // 2, :, lo + ch : lo + 2 * ch] = a.astype(act.dtype)
        act[s, row // 2, :, lo + 2 * ch : lo + 3 * ch] = pad[slot, 9 : 9 + wc].astype(act.dtype)

    def norm_frame(phase, s, own):
        for row in range(hr + 2):
            if phase == 0:
                x = ext[s, row].astype(jnp.float32)
            elif not own or row in (0, hr + 1):
                x = ext2[s, row].astype(jnp.float32)
            else:
                q = row - 1
                x = mid[s - 2, q // 2, :, (q % 2) * ch : (q % 2 + 1) * ch]
            norm_row(x, phase, s, row, own)

    def product(layer, s, w):
        lhs = jnp.concatenate(
            [act[s, half : half + pairs].reshape(pairs * wc, 6 * ch) for half in range(2)], axis=1
        )
        return jnp.dot(lhs, wpair[layer, w], preferred_element_type=jnp.float32)

    def source(f, k):
        return f + 2 - jnp.minimum(2 - k, pos[f])

    def conv_own(layer):
        norm_frame(layer, 5, True)
        acc[3] = product(layer, 5, 2)
        norm_frame(layer, 4, True)
        acc[3] = acc[3] + product(layer, 4, 1)
        acc[2] = product(layer, 4, 2)
        norm_frame(layer, 3, True)
        acc[1] = product(layer, 3, 2)
        norm_frame(layer, 2, True)
        acc[0] = product(layer, 2, 2)
        acc[3] = acc[3] + product(layer, source(3, 0), 0)
        acc[2] = acc[2] + product(layer, source(2, 1), 1) + product(layer, source(2, 0), 0)
        acc[1] = acc[1] + product(layer, source(1, 1), 1)

    def conv_prev(layer):
        norm_frame(layer, 1, False)
        acc[1] = acc[1] + product(layer, source(1, 0), 0)
        norm_frame(layer, 0, False)
        acc[0] = acc[0] + product(layer, source(0, 1), 1) + product(layer, source(0, 0), 0)

    def column_sums(x):
        return jnp.sum(x, axis=0, keepdims=True)

    loads[0].wait()
    @pl.loop(0, nf)
    def _(f):
        one = jnp.zeros((8, ch), jnp.float32)
        two = jnp.zeros((8, ch), jnp.float32)
        for row in range(1, hr + 1):
            x = ext[f + 2, row].astype(jnp.float32).reshape(wc // 8, 8, ch)
            one = one + jnp.sum(x, axis=0)
            two = two + jnp.sum(x * x, axis=0)
        stat[0, pl.ds(f, 1)] = column_sums(one)
        stat[0, pl.ds(f + nf, 1)] = column_sums(two)

    pl.semaphore_wait(barrier, near_n - 1 + 2 * far_n - 1 + 4)
    sum_start(0)

    halos = [
        send(frames.at[:, hr - 1], ext.at[2 : 2 + nf, 0], 6, t, below),
        send(frames.at[:, 0], ext.at[2 : 2 + nf, hr + 1], 7, t, above),
        send(frames.at[nf - 2 : nf, hr - 1], ext.at[0:2, 0], 8, after, below),
        send(frames.at[nf - 2 : nf, 0], ext.at[0:2, hr + 1], 9, after, above),
        send(frames.at[nf - 2 : nf], ext.at[0:2, 1 : 1 + hr], 10, after, r),
    ]
    for halo in halos:
        halo.start()

    loads[1].wait()
    fill_weights(0)
    for slot in range(hr + 2):
        pad[slot, 0:8] = jnp.zeros((8, ch), jnp.float32)
        pad[slot, 8 + wc : 16 + wc] = jnp.zeros((8, ch), jnp.float32)
    sum_middle(0)
    loads[2].wait()
    fill_weights(1)
    for load in loads[3:]:
        load.wait()
    own_affine(0)
    halos[0].wait_recv()
    halos[1].wait_recv()
    conv_own(0)

    def middle_done(f):
        total = acc[f].reshape(pairs, wc, 2 * ch)
        mid[f] = total
        one = jnp.sum(total.reshape(pairs * wc // 8, 8, 2 * ch), axis=0)
        two = jnp.sum((total * total).reshape(pairs * wc // 8, 8, 2 * ch), axis=0)
        one = column_sums(one[:, :ch] + one[:, ch:])
        two = column_sums(two[:, :ch] + two[:, ch:])
        stat[1, f : f + 1] = one
        stat[1, f + nf : f + nf + 1] = two
        for row in range(hr):
            if f >= nf - 2 or row in (0, hr - 1):
                own2[f, row] = total[row // 2, :, (row % 2) * ch : (row % 2 + 1) * ch].astype(own2.dtype)

    def send_middle(first):
        sends = [
            send(own2.at[nf - 2 : nf, hr - 1], ext2.at[0:2, 0], first, after, below),
            send(own2.at[nf - 2 : nf, 0], ext2.at[0:2, hr + 1], first + 1, after, above),
            send(own2.at[nf - 2 : nf], ext2.at[0:2, 1 : 1 + hr], first + 2, after, r),
        ]
        for each in sends:
            each.start()
        return sends

    middle_done(3)
    middle_done(2)
    halos2 = send_middle(11)
    prev_affine(0)
    for halo in halos[2:]:
        halo.wait_recv()
    conv_prev(0)
    for f in (1, 0):
        middle_done(f)
    sum_start(1)
    edges2 = [
        send(own2.at[:, hr - 1], ext2.at[2 : 2 + nf, 0], 17, t, below),
        send(own2.at[:, 0], ext2.at[2 : 2 + nf, hr + 1], 18, t, above),
    ]
    for edge in edges2:
        edge.start()
    sum_middle(1)
    own_affine(1)
    for edge in edges2:
        edge.wait_recv()
    conv_own(1)

    def output_done(f):
        total = acc[f].reshape(pairs, wc, 2 * ch)
        for row in range(hr):
            piece = total[row // 2, :, (row % 2) * ch : (row % 2 + 1) * ch]
            kept = ext[f + 2, row + 1].astype(jnp.float32)
            out[f, row] = (kept + piece).astype(out.dtype)

    output_done(3)
    output_done(2)
    prev_affine(1)
    for halo in halos2:
        halo.wait_recv()
    conv_prev(1)
    for f in (1, 0):
        output_done(f)
    for sent in halos + halos2 + edges2:
        sent.wait_send()
    sum_drain(0)
    sum_drain(1)

def body(frames, video_pos, gain1, shift1, weight1, gain2, shift2, weight2):
    nt = lax.axis_size("tm")
    nr = lax.axis_size("rows")
    nf, hr, wc, ch = frames.shape
    near_n = near_size(nr)
    far_n = nr // near_n
    bf, f32 = jnp.bfloat16, jnp.float32
    hbm = pl.BlockSpec(memory_space=pltpu.HBM)
    call = pl.pallas_call(
        functools.partial(kernel, nt, nr),
        out_shape=pltpu.VMEM(frames.shape, frames.dtype),
        in_specs=[hbm] * 8,
        out_specs=pl.BlockSpec(memory_space=pltpu.VMEM),
        scratch_shapes=[
            pltpu.VMEM((nf + 2, hr + 2, wc, ch), bf),
            pltpu.VMEM((nf + 2, hr + 2, wc, ch), bf),
            pltpu.VMEM((nf, hr, wc, ch), bf),
            pltpu.VMEM((nf, hr // 2, wc, 2 * ch), f32),
            pltpu.VMEM((nf, hr // 2 * wc, 2 * ch), f32),
            pltpu.VMEM((nf + 2, hr // 2 + 1, wc, 6 * ch), bf),
            pltpu.VMEM((hr + 2, wc + 16, ch), f32),
            pltpu.VMEM((2, 27 * ch, ch), bf),
            pltpu.VMEM((2, 3, 12 * ch, 2 * ch), bf),
            pltpu.VMEM((4, 1, ch), f32),
            pltpu.SMEM((nf,), jnp.int32),
            pltpu.VMEM((2, 2, 2, 8, ch), f32),
            pltpu.VMEM((2, 2 * nf, ch), f32),
            pltpu.VMEM((2, 2, ch), f32),
            pltpu.VMEM((2, 2, ch), f32),
            pltpu.VMEM((2, near_n, 2, ch), f32),
            pltpu.VMEM((2, far_n, 2, ch), f32),
            pltpu.VMEM((2, far_n, 2, ch), f32),
            pltpu.SemaphoreType.DMA((8,)),
            pltpu.SemaphoreType.DMA((19,)),
            pltpu.SemaphoreType.DMA((19,)),
        ],
        compiler_params=pltpu.CompilerParams(
            collective_id=0, has_side_effects=True, vmem_limit_bytes=40 * 1024 * 1024
        ),
        name="encoder_block",
    )
    operands = (
        frames,
        video_pos,
        gain1.reshape(1, ch),
        shift1.reshape(1, ch),
        weight1.reshape(27 * ch, ch),
        gain2.reshape(1, ch),
        shift2.reshape(1, ch),
        weight2.reshape(27 * ch, ch),
    )
    return call(*(pltpu.with_memory_space_constraint(x, pltpu.HBM) for x in operands))


def solution(mesh):
    placed = (P("tm", "rows", None, None), P("tm"), P(), P(), P(), P(), P(), P())
    return jax.shard_map(
        body, mesh=mesh, in_specs=placed, out_specs=P("tm", "rows", None, None), check_vma=False
    )
```

time: 53 us -> 41.7 us (0.79)
  Pallas kernels: 47.8 us -> 40.8 us
  local copies, waits for them, and re-layouts: 4.87 us -> 0.8 us
    pallas_call x1, Pallas kernels: 47.8 us -> 40.8 us  [body(): call(*(pltpu.with_memory_space_constraint(x, pltpu.HBM) for x in operands))]
    unnamed x17 -> x1, local copies, waits for them, and re-layouts: 4.87 us -> 0.8 us
where the time goes in v2:
time: 41.7 us; the launch traced here: 41.6 us
  Pallas kernels  40.8 us (98%)
  local copies, waits for them, and re-layouts  0.8 us (2%)
    pallas_call x1, Pallas kernels, body(): call(*(pltpu.with_memory_space_constraint(x, pltpu.HBM) for x in operands))  40.8 us

profile of v2, /device:TPU:1, one launch (start us, length us, event | category | flops | bytes accessed | tf_op | source)
XLA Modules:
  0.0 41.6 jit_solution(7330682331077294051)
XLA Ops:
  0.0 40.8 %encoder_block.1 = bf16[4,8,64,128]{3,2,1,0:T(8,128)(2,1)S(1)} custom-call(bf16[4,8,64,128]{3,2,1,0:T(8,128)(2,1)} %frames.1, s32[4]{0:T(128)} %video_pos.1, f32[1,128]{1,0:T(1,128)} %bitcast.8, f32[1,128]{1,0:T(1,128)} %bitcast.9, bf16[3456,128]{1,0:T(8,128)(2,1)} %bitcast.6, f32[1,128]{1,0:T(1,128)} %bitcast.10, f32[1,128]{1,0:T(1,128)} %bitcast.11, ...), custom_call_target="tpu_custom_call" | custom-call | tf_op jit(solution)/shard_map/encoder_block/pallas_call | solution.py:419
  40.8 0.8 %copy.10 = bf16[4,8,64,128]{3,2,1,0:T(8,128)(2,1)} copy(bf16[4,8,64,128]{3,2,1,0:T(8,128)(2,1)S(1)} %encoder_block.1) | data formatting | bytes 1048576

commit v3 on v2

--- a/solution.py
+++ b/solution.py
@@ -37,7 +37,8 @@
     mid,
     acc,
     act,
-    pad,
+    raw,
+    turn,
     wraw,
     wpair,
     params,
@@ -202,25 +203,33 @@
         jnp.where(r < nr - 1, 1.0, 0.0).astype(jnp.float32),
     )
 
+    eight = lax.broadcasted_iota(jnp.int32, (8, ch), 0)
+
     def norm_row(x, phase, s, row, own):
         f = s - 2 if own else s + nf - 2
-        slot = row
         y = x * affine[phase, int(own), 0, pl.ds(f, 1)] + affine[phase, int(own), 1, pl.ds(f, 1)]
         a = y * (0.5 * jnp.tanh(0.5 * y) + 0.5)
         if row == 0:
             a = a * row_ok[0]
         if row == hr + 1:
             a = a * row_ok[1]
-        pad[slot, 8 : 8 + wc] = a
+        first = jnp.where(eight == 0, 0.0, pltpu.roll(a[wc - 8 :], 1, 0))
+        last = jnp.where(eight == 7, 0.0, pltpu.roll(a[:8], 7, 0))
         lo = (row % 2) * 3 * ch
-        act[s, row // 2, :, lo : lo + ch] = pad[slot, 7 : 7 + wc].astype(act.dtype)
+        act[s, row // 2, :, lo : lo + ch] = jnp.concatenate([first, a[: wc - 8]], axis=0).astype(act.dtype)
         act[s, row // 2, :, lo + ch : lo + 2 * ch] = a.astype(act.dtype)
-        act[s, row // 2, :, lo + 2 * ch : lo + 3 * ch] = pad[slot, 9 : 9 + wc].astype(act.dtype)
+        act[s, row // 2, :, lo + 2 * ch : lo + 3 * ch] = jnp.concatenate([a[8:], last], axis=0).astype(act.dtype)
+
+    def permute(s, rows):
+        for row in rows:
+            turn[row] = ext[s, row].astype(jnp.float32)
+            for j in range(8):
+                raw[s, row, 8 * j : 8 * j + 8] = turn[row, pl.ds(j, 8, stride=8)]
 
     def norm_frame(phase, s, own):
         for row in range(hr + 2):
             if phase == 0:
-                x = ext[s, row].astype(jnp.float32)
+                x = raw[s, row]
             elif not own or row in (0, hr + 1):
                 x = ext2[s, row].astype(jnp.float32)
             else:
@@ -287,17 +296,24 @@
 
     loads[1].wait()
     fill_weights(0)
-    for slot in range(hr + 2):
-        pad[slot, 0:8] = jnp.zeros((8, ch), jnp.float32)
-        pad[slot, 8 + wc : 16 + wc] = jnp.zeros((8, ch), jnp.float32)
+
+    @pl.loop(2, 2 + nf)
+    def _(s):
+        permute(s, range(1, 1 + hr))
+
     sum_middle(0)
     loads[2].wait()
     fill_weights(1)
     for load in loads[3:]:
         load.wait()
-    own_affine(0)
     halos[0].wait_recv()
     halos[1].wait_recv()
+
+    @pl.loop(2, 2 + nf)
+    def _(s):
+        permute(s, (0, hr + 1))
+
+    own_affine(0)
     conv_own(0)
 
     def middle_done(f):
@@ -329,6 +345,11 @@
     prev_affine(0)
     for halo in halos[2:]:
         halo.wait_recv()
+
+    @pl.loop(0, 2)
+    def _(s):
+        permute(s, range(hr + 2))
+
     conv_prev(0)
     for f in (1, 0):
         middle_done(f)
@@ -349,8 +370,10 @@
         total = acc[f].reshape(pairs, wc, 2 * ch)
         for row in range(hr):
             piece = total[row // 2, :, (row % 2) * ch : (row % 2 + 1) * ch]
+            for j in range(8):
+                turn[row, pl.ds(j, 8, stride=8)] = piece[8 * j : 8 * j + 8]
             kept = ext[f + 2, row + 1].astype(jnp.float32)
-            out[f, row] = (kept + piece).astype(out.dtype)
+            out[f, row] = (kept + turn[row]).astype(out.dtype)
 
     output_done(3)
     output_done(2)
@@ -385,7 +408,8 @@
             pltpu.VMEM((nf, hr // 2, wc, 2 * ch), f32),
             pltpu.VMEM((nf, hr // 2 * wc, 2 * ch), f32),
             pltpu.VMEM((nf + 2, hr // 2 + 1, wc, 6 * ch), bf),
-            pltpu.VMEM((hr + 2, wc + 16, ch), f32),
+            pltpu.VMEM((nf + 2, hr + 2, wc, ch), f32),
+            pltpu.VMEM((hr + 2, wc, ch), f32),
             pltpu.VMEM((2, 27 * ch, ch), bf),
             pltpu.VMEM((2, 3, 12 * ch, 2 * ch), bf),
             pltpu.VMEM((4, 1, ch), f32),

time: 41.7 us -> 41.4 us (level)
  no operation moved by 1% of the time
where the time goes in v3:
time: 41.4 us; the launch traced here: 41.2 us
  Pallas kernels  40.4 us (98%)
  local copies, waits for them, and re-layouts  0.8 us (2%)
    pallas_call x1, Pallas kernels, body(): call(*(pltpu.with_memory_space_constraint(x, pltpu.HBM) for x in operands))  40.4 us

profile of v3, /device:TPU:1, one launch (start us, length us, event | category | flops | bytes accessed | tf_op | source)
XLA Modules:
  0.0 41.2 jit_solution(7533008485351130116)
XLA Ops:
  0.0 40.4 %encoder_block.1 = bf16[4,8,64,128]{3,2,1,0:T(8,128)(2,1)S(1)} custom-call(bf16[4,8,64,128]{3,2,1,0:T(8,128)(2,1)} %frames.1, s32[4]{0:T(128)} %video_pos.1, f32[1,128]{1,0:T(1,128)} %bitcast.8, f32[1,128]{1,0:T(1,128)} %bitcast.9, bf16[3456,128]{1,0:T(8,128)(2,1)} %bitcast.6, f32[1,128]{1,0:T(1,128)} %bitcast.10, f32[1,128]{1,0:T(1,128)} %bitcast.11, ...), custom_call_target="tpu_custom_call" | custom-call | tf_op jit(solution)/shard_map/encoder_block/pallas_call | solution.py:443
  40.4 0.8 %copy.10 = bf16[4,8,64,128]{3,2,1,0:T(8,128)(2,1)} copy(bf16[4,8,64,128]{3,2,1,0:T(8,128)(2,1)S(1)} %encoder_block.1) | data formatting | bytes 1048576

commit v4 on v3

--- a/solution.py
+++ b/solution.py
@@ -34,7 +34,6 @@
     ext,
     ext2,
     own2,
-    mid,
     acc,
     act,
     raw,
@@ -68,6 +67,9 @@
     after = lax.rem(t + 1, nt)
     before = lax.rem(t + nt - 1, nt)
 
+    def far_first(n):
+        return sorted(range(1, n), key=lambda step: -min(step, n - step))
+
     def near_peer(step):
         return in_far * near_n + lax.rem(in_near + step, near_n)
 
@@ -75,7 +77,6 @@
         return lax.rem(in_far + step, far_n) * near_n + in_near
 
     loads = [
-        pltpu.make_async_copy(frames, ext.at[2 : 2 + nf, 1 : 1 + hr], load_sem.at[0]),
         pltpu.make_async_copy(weight1, wraw.at[0], load_sem.at[1]),
         pltpu.make_async_copy(weight2, wraw.at[1], load_sem.at[2]),
         pltpu.make_async_copy(video_pos, pos, load_sem.at[3]),
@@ -84,7 +85,11 @@
         pltpu.make_async_copy(gain2, params.at[2], load_sem.at[6]),
         pltpu.make_async_copy(shift2, params.at[3], load_sem.at[7]),
     ]
-    for load in loads:
+    frame_loads = [
+        pltpu.make_async_copy(frames.at[f], ext.at[f + 2, 1 : 1 + hr], load_sem.at[8 + f])
+        for f in range(nf)
+    ]
+    for load in frame_loads + loads:
         load.start()
 
     barrier = pltpu.get_barrier_semaphore()
@@ -92,16 +97,11 @@
     def greet(tt, rr):
         pl.semaphore_signal(barrier, inc=1, device_id=(tt, rr), device_id_type=MESH)
 
-    @pl.loop(1, near_n)
-    def _(step):
+    for step in far_first(far_n):
+        greet(t, far_peer(step))
+    for step in far_first(near_n):
         greet(t, near_peer(step))
-
-    @pl.loop(1, far_n)
-    def _(step):
-        greet(t, far_peer(step))
-
-    @pl.loop(0, far_n)
-    def _(step):
+    for step in far_first(far_n) + [0]:
         greet(before, far_peer(step))
 
     greet(t, above)
@@ -136,8 +136,7 @@
         packed[phase] = jnp.concatenate([one, two], axis=0)
         near[phase, in_near] = packed[phase]
 
-        @pl.loop(1, near_n)
-        def _(step):
+        for step in far_first(near_n):
             send(
                 packed.at[phase], near.at[phase, in_near], 3 * phase, t, near_peer(step)
             ).start()
@@ -151,14 +150,12 @@
         part[phase] = total
         far[phase, in_far] = total
 
-        @pl.loop(1, far_n)
-        def _(step):
+        for step in far_first(far_n):
             send(
                 part.at[phase], far.at[phase, in_far], 3 * phase + 1, t, far_peer(step)
             ).start()
 
-        @pl.loop(0, far_n)
-        def _(step):
+        for step in far_first(far_n) + [0]:
             send(
                 part.at[phase], prev.at[phase, in_far], 3 * phase + 2, after, far_peer(step)
             ).start()
@@ -234,7 +231,7 @@
                 x = ext2[s, row].astype(jnp.float32)
             else:
                 q = row - 1
-                x = mid[s - 2, q // 2, :, (q % 2) * ch : (q % 2 + 1) * ch]
+                x = acc[s - 2, (q // 2) * wc : (q // 2 + 1) * wc, (q % 2) * ch : (q % 2 + 1) * ch]
             norm_row(x, phase, s, row, own)
 
     def product(layer, s, w):
@@ -269,17 +266,16 @@
     def column_sums(x):
         return jnp.sum(x, axis=0, keepdims=True)
 
-    loads[0].wait()
-    @pl.loop(0, nf)
-    def _(f):
+    for f in range(nf):
+        frame_loads[f].wait()
         one = jnp.zeros((8, ch), jnp.float32)
         two = jnp.zeros((8, ch), jnp.float32)
         for row in range(1, hr + 1):
             x = ext[f + 2, row].astype(jnp.float32).reshape(wc // 8, 8, ch)
             one = one + jnp.sum(x, axis=0)
             two = two + jnp.sum(x * x, axis=0)
-        stat[0, pl.ds(f, 1)] = column_sums(one)
-        stat[0, pl.ds(f + nf, 1)] = column_sums(two)
+        stat[0, f : f + 1] = column_sums(one)
+        stat[0, f + nf : f + nf + 1] = column_sums(two)
 
     pl.semaphore_wait(barrier, near_n - 1 + 2 * far_n - 1 + 4)
     sum_start(0)
@@ -294,7 +290,7 @@
     for halo in halos:
         halo.start()
 
-    loads[1].wait()
+    loads[0].wait()
     fill_weights(0)
 
     @pl.loop(2, 2 + nf)
@@ -302,9 +298,9 @@
         permute(s, range(1, 1 + hr))
 
     sum_middle(0)
-    loads[2].wait()
+    loads[1].wait()
     fill_weights(1)
-    for load in loads[3:]:
+    for load in loads[2:]:
         load.wait()
     halos[0].wait_recv()
     halos[1].wait_recv()
@@ -318,7 +314,6 @@
 
     def middle_done(f):
         total = acc[f].reshape(pairs, wc, 2 * ch)
-        mid[f] = total
         one = jnp.sum(total.reshape(pairs * wc // 8, 8, 2 * ch), axis=0)
         two = jnp.sum((total * total).reshape(pairs * wc // 8, 8, 2 * ch), axis=0)
         one = column_sums(one[:, :ch] + one[:, ch:])
@@ -405,7 +400,6 @@
             pltpu.VMEM((nf + 2, hr + 2, wc, ch), bf),
             pltpu.VMEM((nf + 2, hr + 2, wc, ch), bf),
             pltpu.VMEM((nf, hr, wc, ch), bf),
-            pltpu.VMEM((nf, hr // 2, wc, 2 * ch), f32),
             pltpu.VMEM((nf, hr // 2 * wc, 2 * ch), f32),
             pltpu.VMEM((nf + 2, hr // 2 + 1, wc, 6 * ch), bf),
             pltpu.VMEM((nf + 2, hr + 2, wc, ch), f32),
@@ -421,7 +415,7 @@
             pltpu.VMEM((2, near_n, 2, ch), f32),
             pltpu.VMEM((2, far_n, 2, ch), f32),
             pltpu.VMEM((2, far_n, 2, ch), f32),
-            pltpu.SemaphoreType.DMA((8,)),
+            pltpu.SemaphoreType.DMA((12,)),
             pltpu.SemaphoreType.DMA((19,)),
             pltpu.SemaphoreType.DMA((19,)),
         ],

time: 41.4 us -> 41 us (level)
  no operation moved by 1% of the time
where the time goes in v4:
time: 41 us; the launch traced here: 40.8 us
  Pallas kernels  40 us (98%)
  local copies, waits for them, and re-layouts  0.8 us (2%)
    pallas_call x1, Pallas kernels, body(): call(*(pltpu.with_memory_space_constraint(x, pltpu.HBM) for x in operands))  40 us

profile of v4, /device:TPU:1, one launch (start us, length us, event | category | flops | bytes accessed | tf_op | source)
XLA Modules:
  0.0 40.8 jit_solution(2116169850489945420)
XLA Ops:
  0.0 40.0 %encoder_block.1 = bf16[4,8,64,128]{3,2,1,0:T(8,128)(2,1)S(1)} custom-call(bf16[4,8,64,128]{3,2,1,0:T(8,128)(2,1)} %frames.1, s32[4]{0:T(128)} %video_pos.1, f32[1,128]{1,0:T(1,128)} %bitcast.8, f32[1,128]{1,0:T(1,128)} %bitcast.9, bf16[3456,128]{1,0:T(8,128)(2,1)} %bitcast.6, f32[1,128]{1,0:T(1,128)} %bitcast.10, f32[1,128]{1,0:T(1,128)} %bitcast.11, ...), custom_call_target="tpu_custom_call" | custom-call | tf_op jit(solution)/shard_map/encoder_block/pallas_call | solution.py:437
  40.0 0.8 %copy.10 = bf16[4,8,64,128]{3,2,1,0:T(8,128)(2,1)} copy(bf16[4,8,64,128]{3,2,1,0:T(8,128)(2,1)S(1)} %encoder_block.1) | data formatting | bytes 1048576

commit v5 on v4

--- a/solution.py
+++ b/solution.py
@@ -89,7 +89,7 @@
         pltpu.make_async_copy(frames.at[f], ext.at[f + 2, 1 : 1 + hr], load_sem.at[8 + f])
         for f in range(nf)
     ]
-    for load in frame_loads + loads:
+    for load in frame_loads:
         load.start()
 
     barrier = pltpu.get_barrier_semaphore()
@@ -108,6 +108,9 @@
     greet(t, below)
     greet(before, above)
     greet(before, below)
+
+    for load in loads:
+        load.start()
 
     def send(src, dst, which, tt, rr):
         return pltpu.make_async_remote_copy(

time: 41 us -> 41 us (level)
  no operation moved by 1% of the time
where the time goes in v5:
time: 41 us; the launch traced here: 40.8 us
  Pallas kernels  40 us (98%)
  local copies, waits for them, and re-layouts  0.8 us (2%)
    pallas_call x1, Pallas kernels, body(): call(*(pltpu.with_memory_space_constraint(x, pltpu.HBM) for x in operands))  40 us

profile of v5, /device:TPU:1, one launch (start us, length us, event | category | flops | bytes accessed | tf_op | source)
XLA Modules:
  0.0 40.8 jit_solution(8558081620227644369)
XLA Ops:
  0.0 40.0 %encoder_block.1 = bf16[4,8,64,128]{3,2,1,0:T(8,128)(2,1)S(1)} custom-call(bf16[4,8,64,128]{3,2,1,0:T(8,128)(2,1)} %frames.1, s32[4]{0:T(128)} %video_pos.1, f32[1,128]{1,0:T(1,128)} %bitcast.8, f32[1,128]{1,0:T(1,128)} %bitcast.9, bf16[3456,128]{1,0:T(8,128)(2,1)} %bitcast.6, f32[1,128]{1,0:T(1,128)} %bitcast.10, f32[1,128]{1,0:T(1,128)} %bitcast.11, ...), custom_call_target="tpu_custom_call" | custom-call | tf_op jit(solution)/shard_map/encoder_block/pallas_call | solution.py:440
  40.0 0.8 %copy.10 = bf16[4,8,64,128]{3,2,1,0:T(8,128)(2,1)} copy(bf16[4,8,64,128]{3,2,1,0:T(8,128)(2,1)S(1)} %encoder_block.1) | data formatting | bytes 1048576
